TPU v7x, 128 devices: a whole 4x4x4 slice. The times are simulated.
128 devices in a mesh: row: 8 (over y, core), col: 16 (over z, x).
Axes of the slice: x: 4, y: 4, z: 4, core: 2. Of those that a mesh axis runs over, the one named last changes fastest.
Arguments:
- child_fronts: float32 [20, 512, 20, 1024], P(None, 'col', None, 'row'), as said below
- parent_diagonal: float32 [16384], replicated, may hold values from 0.5 to 4
- block_maps: int32 [2, 20], replicated, may hold values from 0 to 31, as said below
Outputs:
- factored: float32 [16384, 16384], P('row', 'col')
Inputs may be any that keep to these rules, and one draw needn't show every extreme that they name: `child_fronts`: each child's matrix is symmetric and positive definite. `block_maps`: each row names 20 distinct front blocks in increasing order; every one of the 32 front blocks is named by at least one row, and exactly 8 of them by both rows.
All inputs are finite; a program needn't handle non-finite values.
Results may differ from a plain program's by a relative error of at most 0.0001.
Values sent between devices are 32-bit elements; how exact they have to be, the bound alone decides.
No kernel may reach another device: no remote copies, remote signals or barrier semaphores. Data moves between devices by JAX's collectives and lax.ppermute only.
A program may use at most 128 MiB of HBM per device.

v0:
```python
import jax
import jax.numpy as jnp
from jax import lax
from jax.sharding import PartitionSpec as P

B = 512


def broadcast(x, axis, root):
    mine = lax.axis_index(axis) == root
    return lax.psum(jnp.where(mine, x, jnp.zeros_like(x)), axis)


def inverse_maps(block_maps, count):
    blocks = jnp.arange(count, dtype=jnp.int32)
    matches = block_maps[:, None, :] == blocks[None, :, None]
    present = jnp.any(matches, axis=2)
    places = jnp.arange(block_maps.shape[1], dtype=jnp.int32)
    source = jnp.sum(jnp.where(matches, places[None, None, :], 0), axis=2)
    return (source, present)


def shards(child_fronts, parent_diagonal, block_maps):
    row_count = lax.axis_size("row")
    column_count = lax.axis_size("col")
    row_index = lax.axis_index("row")
    column_index = lax.axis_index("col")
    half_count = row_count // 2
    blocks = parent_diagonal.shape[0] // B
    local_rows = blocks // row_count
    local_cols = blocks // column_count
    slice_rows = B // column_count
    slice_cols = 2 * B // row_count
    source, present = inverse_maps(block_maps, blocks)
    my_child = row_index // half_count
    my_source = lax.dynamic_index_in_dim(source, my_child, 0, keepdims=False)
    my_present = lax.dynamic_index_in_dim(present, my_child, 0, keepdims=False)
    picked_rows = jnp.take(child_fronts, my_source, axis=0)
    picked_both = jnp.take(picked_rows, my_source, axis=2)
    keep_mask = my_present[:, None, None, None] & my_present[None, None, :, None]
    picked_both = jnp.where(keep_mask, picked_both, 0.0)
    buffer = picked_both.reshape(
        local_rows, row_count, slice_rows, local_cols, column_count, slice_cols
    )
    buffer = buffer.transpose(1, 4, 0, 2, 3, 5).reshape(row_count * column_count, -1)
    received = lax.all_to_all(buffer, ("row", "col"), split_axis=0, concat_axis=0, tiled=True)
    received = received.reshape(
        2, half_count, column_count, local_rows, slice_rows, local_cols, slice_cols
    )
    summed = received[0] + received[1]
    frontal = summed.transpose(2, 1, 3, 4, 0, 5).reshape(local_rows, B, local_cols, B)
    row_blocks = jnp.arange(local_rows, dtype=jnp.int32) * row_count + row_index
    col_blocks = jnp.arange(local_cols, dtype=jnp.int32) * column_count + column_index
    diag_table = parent_diagonal.reshape(blocks, B)
    diag_rows = jnp.take(diag_table, row_blocks, axis=0)
    same_block = row_blocks[:, None] == col_blocks[None, :]
    identity = jnp.arange(B)[:, None] == jnp.arange(B)[None, :]
    diag_mask = same_block[:, None, :, None] & identity[None, :, None, :]
    frontal = frontal + jnp.where(diag_mask, diag_rows[:, :, None, None], 0.0)
    for panel_index in range(2):
        column_slab = frontal[:, :, panel_index // column_count, :]
        root_row = panel_index % row_count
        local_row = panel_index // row_count
        root_col = panel_index % column_count
        diagonal = broadcast(column_slab[local_row], "row", root_row)
        lower_factor = jnp.linalg.cholesky(diagonal)
        solved = jax.scipy.linalg.solve_triangular(
            lower_factor, column_slab.reshape(-1, B).T, lower=True
        ).T
        solved = solved.reshape(local_rows, B, B)
        factor_factor_column = jnp.where(
            (row_blocks > panel_index)[:, None, None],
            solved,
            jnp.where((row_blocks == panel_index)[:, None, None], lower_factor[None], 0.0),
        )
        factor_factor_column = broadcast(factor_factor_column, "col", root_col)
        owner_rows = (
            jnp.arange(local_cols, dtype=jnp.int32) * column_count + column_index
        ) // row_count
        factor_picked_rows = jnp.take(factor_factor_column, owner_rows, axis=0)
        factor_across = broadcast(factor_picked_rows, "row", column_index % row_count)
        section = frontal
        span_count = local_cols - 0
        product = lax.dot_general(
            factor_factor_column.reshape(-1, B),
            factor_across.reshape(-1, B),
            (((1,), (1,)), ((), ())),
            precision=lax.Precision.HIGHEST,
            preferred_element_type=jnp.float32,
        )
        product = product.reshape(local_rows, B, span_count, B)
        inside = (row_blocks > panel_index)[:, None, None, None] & (col_blocks > panel_index)[
            None, None, :, None
        ]
        section = jnp.where(inside, section - product, section)
        section = jnp.where(
            (col_blocks == panel_index)[None, None, :, None],
            factor_factor_column[:, :, None, :],
            section,
        )
        upper_mask = (row_blocks == panel_index)[:, None, None, None] & (col_blocks > panel_index)[
            None, None, :, None
        ]
        section = jnp.where(upper_mask, 0.0, section)
        frontal = frontal.at[:, :, 0:local_cols, :].set(section)
    return frontal.reshape(local_rows * B, local_cols * B)


def solution(mesh):
    return jax.shard_map(
        shards,
        mesh=mesh,
        in_specs=(P(None, "col", None, "row"), P(), P()),
        out_specs=P("row", "col"),
        check_vma=False,
    )
```

profile of v0, /device:TPU:0, one launch (start us, length us, event | category | flops | bytes accessed | tf_op | source)
XLA Modules:
  0.0 1235.0 jit_solution(6929566411655299351)
XLA Ops:
  7.6 8.1 gather_fusion
  15.6 10.1 broadcast_select_fusion
  25.7 12.2 gather_fusion.1
  38.7 29.2 %fusion = f32[4,8,32,2,16,128]{5,3,2,0,4,1:T(2,128)} fusion(f32[4,8,32,2,16,128]{5,2,1,0,4,3:T(8,128)} %bitcast.155, pred[2,16]{0,1:T(8,128)(4,1)S(1)} %copy.53, pred[4,8,2,16]{2,0,3,1:T(4,128)(4,1)S(1)} %broadcast_and_fusion), kind=kLoop, calls=%fused_computation.10 | loop fusion | flops 8388608 | bytes 33555488 | tf_op jit(solution)/shard_map/jit(_where)/select_n | solution.py:41
  67.9 11.7 all-to-all-start
  80.8 231.2 %all-to-all-done = f32[128,1,32768]{2,1,0:T(1,128)} async-done(((f32[128,1,32768]{2,1,0:T(1,128)}), f32[128,1,32768]{2,1,0:T(1,128)}, u32[]{:S(2)}, u32[]{:S(2)}) %all-to-all-start) | async-done | bytes 16777248 | tf_op jit(solution)/shard_map/all_to_all | solution.py:46
  312.0 11.0 slice_add_fusion
  323.0 12.1 copy.56
  335.1 10.3 reshape.505
  345.4 9.9 copy.57
  369.1 5.2 copy.59
  374.3 5.9 copy.60
  380.2 59.8 %all-reduce.8.cloned.1.call-done = f32[512,512]{0,1:T(8,128)} async-done(((f32[512,512]{0,1:T(8,128)}), f32[512,512]{0,1:T(8,128)}) %all-reduce.8.cloned.1.call-update) | async-done | bytes 1048592 | tf_op jit(solution)/shard_map/psum | solution.py:11
  443.1 11.7 cholesky.286
  455.0 9.8 custom-call.27
  465.5 11.7 cholesky.305
  477.2 10.0 custom-call.28
  487.9 11.7 cholesky.326
  500.3 9.8 custom-call.29
  510.7 11.7 cholesky.343
  527.0 7.8 while.8
  534.8 39.3 %custom-call.30 = f32[4,128,128]{1,2,0:T(8,128)S(1)} custom-call(f32[4,128,128]{2,1,0:T(8,128)S(1)} %get-tuple-element.62), custom_call_target="InvertDiagBlocksLowerTriangular" | custom-call | tf_op jit(solution)/shard_map/jit(_solve_triangular)/triangular_solve | solution.py:67
  587.8 5.3 copy.75
  593.1 4.9 select_select_fusion.1
  598.1 102.9 %all-reduce.10.cloned.1.call-done = f32[4,512,512]{2,1,0:T(8,128)} async-done(((f32[4,512,512]{2,1,0:T(8,128)}), f32[4,512,512]{2,1,0:T(8,128)}) %all-reduce.10.cloned.1.call-update) | async-done | bytes 4194320 | tf_op jit(solution)/shard_map/psum | solution.py:11
  705.8 5.2 copy.62
  711.1 60.1 %all-reduce.12.cloned.1.call-done = f32[2,512,512]{2,1,0:T(8,128)} async-done(((f32[2,512,512]{2,1,0:T(8,128)}), f32[2,512,512]{2,1,0:T(8,128)}) %all-reduce.12.cloned.1.call-update) | async-done | bytes 2097168 | tf_op jit(solution)/shard_map/psum | solution.py:11
  771.2 17.6 %fusion.2 = f32[4,512,2,512]{1,3,2,0:T(8,128)S(1)} fusion(f32[4,512,2,512]{1,3,2,0:T(8,128)} %copy-done, f32[4,512,512]{1,2,0:T(8,128)} %copy.62, pred[2]{0:T(512)(128)(4,1)S(1)} %get-tuple-element.118, pred[4,2]{1,0:T(4,128)(4,1)S(1)} %get-tuple-element.111, pred[4,2]{1,0:T(4,128)(4,1)S(1)} %get-tuple-element.110, ...), kind=kOutput, calls=%fused_computation.14 | convolution fusion | flops 12893290496 | bytes 27262994 | tf_op jit(solution)/shard_map/dot_general | solution.py:84
  797.9 5.3 copy.65
  803.2 5.5 copy.66
  808.7 46.8 %all-reduce.14.cloned.1.call-done = f32[512,512]{0,1:T(8,128)} async-done(((f32[512,512]{0,1:T(8,128)}), f32[512,512]{0,1:T(8,128)}) %all-reduce.14.cloned.1.call-update) | async-done | bytes 1048592 | tf_op jit(solution)/shard_map/psum | solution.py:11
  858.5 11.7 cholesky.358
  870.4 9.8 custom-call.31
  880.9 11.7 cholesky.377
  894.0 10.0 custom-call.32
  904.6 11.7 cholesky.398
  917.1 9.8 custom-call.33
  927.5 11.7 cholesky.415
  943.1 7.8 while.9
  950.9 39.3 %custom-call.34 = f32[4,128,128]{1,2,0:T(8,128)S(1)} custom-call(f32[4,128,128]{2,1,0:T(8,128)S(1)} %get-tuple-element.63), custom_call_target="InvertDiagBlocksLowerTriangular" | custom-call | tf_op jit(solution)/shard_map/jit(_solve_triangular)/triangular_solve | solution.py:67
  1003.9 5.3 copy.67
  1009.2 4.9 select_select_fusion
  1014.3 102.8 %all-reduce.16.cloned.1.call-done = f32[4,512,512]{2,1,0:T(8,128)} async-done(((f32[4,512,512]{2,1,0:T(8,128)}), f32[4,512,512]{2,1,0:T(8,128)}) %all-reduce.16.cloned.1.call-update) | async-done | bytes 4194320 | tf_op jit(solution)/shard_map/psum | solution.py:11
  1121.9 5.2 copy.68
  1127.1 60.2 %all-reduce.18.cloned.1.call-done = f32[2,512,512]{2,1,0:T(8,128)} async-done(((f32[2,512,512]{2,1,0:T(8,128)}), f32[2,512,512]{2,1,0:T(8,128)}) %all-reduce.18.cloned.1.call-update) | async-done | bytes 2097168 | tf_op jit(solution)/shard_map/psum | solution.py:11
  1187.3 18.7 %fusion.4 = f32[4,512,2,512]{1,3,2,0:T(8,128)} fusion(f32[4,512,2,512]{1,3,2,0:T(8,128)} %copy-done.1, f32[4,512,512]{1,2,0:T(8,128)} %copy.68, pred[2]{0:T(512)(128)(4,1)S(1)} %get-tuple-element.124, pred[4,2]{1,0:T(4,128)(4,1)S(1)} %get-tuple-element.109, pred[4,2]{1,0:T(4,128)(4,1)S(1)} %get-tuple-element.108, ...), kind=kOutput, calls=%fused_computation.16 | convolution fusion | flops 12893290496 | bytes 27262994 | tf_op jit(solution)/shard_map/dot_general | solution.py:84
  1205.9 13.2 %copy.70 = f32[4,512,2,512]{3,2,1,0:T(2,128)} copy(f32[4,512,2,512]{1,3,2,0:T(8,128)} %fusion.4) | data formatting | bytes 16777216 | tf_op jit(solution)/shard_map/jit(_where)/select_n | solution.py:104
  1219.1 8.9 copy.78
  (151 shorter events, 94.5 us)
Async XLA Ops:
  67.9 12.0 copy-start.4
  67.9 244.1 %all-to-all-start = ((f32[128,1,32768]{2,1,0:T(1,128)}), f32[128,1,32768]{2,1,0:T(1,128)}, u32[]{:S(2)}, u32[]{:S(2)}) async-start(f32[128,1,32768]{2,1,0:T(1,128)} %bitcast.154), calls=%async_computation | async-start | bytes 33554432 | tf_op jit(solution)/shard_map/all_to_all | solution.py:46
  79.6 360.5 %all-reduce.8.cloned.1.call-start = ((), (), s32[]{:S(2)}) async-start(), calls=%async_computation.1 | async-start | bytes 2097152 | tf_op jit(solution)/shard_map/psum | solution.py:11
  360.0 3.4 copy-start
  364.5 336.6 %all-reduce.10.cloned.1.call-start = ((), (), s32[]{:S(2)}) async-start(), calls=%async_computation.2 | async-start | bytes 8388608 | tf_op jit(solution)/shard_map/psum | solution.py:11
  574.1 5.7 copy-start.2
  598.0 173.1 %all-reduce.12.cloned.1.call-start = ((), (), s32[]{:S(2)}) async-start(), calls=%async_computation.3 | async-start | bytes 4194304 | tf_op jit(solution)/shard_map/psum | solution.py:11
  705.7 149.8 %all-reduce.14.cloned.1.call-start = ((), (), s32[]{:S(2)}) async-start(), calls=%async_computation.4 | async-start | bytes 2097152 | tf_op jit(solution)/shard_map/psum | solution.py:11
  788.8 3.4 copy-start.1
  793.3 323.8 %all-reduce.16.cloned.1.call-start = ((), (), s32[]{:S(2)}) async-start(), calls=%async_computation.5 | async-start | bytes 8388608 | tf_op jit(solution)/shard_map/psum | solution.py:11
  990.2 5.7 copy-start.3
  1014.1 173.1 %all-reduce.18.cloned.1.call-start = ((), (), s32[]{:S(2)}) async-start(), calls=%async_computation.6 | async-start | bytes 4194304 | tf_op jit(solution)/shard_map/psum | solution.py:11
Sparse Core Ops, SparseCore 0:
  364.6 75.4 all-reduce.7
  598.1 102.8 all-reduce.9
  705.8 65.3 all-reduce.11
  793.4 62.0 all-reduce.13
  1014.2 102.8 all-reduce.15
  1121.9 65.3 all-reduce.17
where the time goes:
time: 1240 us; the launch traced here: 1230 us
  waiting for transfers between devices  664 us (54%)
  other arithmetic  317 us (26%)
  local copies, waits for them, and re-layouts  160 us (13%)
  matrix products  62.2 us (5%)
  between operations  19.3 us (2%)
  starting transfers between devices  12.4 us (1%)
    psum x6, waiting for transfers between devices, broadcast(): return lax.psum(jnp.where(mine, x, jnp.zeros_like(x)), axis)  433 us
    all_to_all x1, waiting for transfers between devices, shards(): lax.all_to_all(buffer, ('row', 'col'), split_axis=0, concat_axis=0, tiled...  231 us
    another operation x29, other arithmetic, shards(): lower_factor = jnp.linalg.cholesky(diagonal)  158 us
    another operation x5, other arithmetic, shards(): jax.scipy.linalg.solve_triangular(lower_factor, column_slab.reshape(-1, B...  79.9 us
    dot_general x2, matrix products, shards(): lax.dot_general(factor_factor_column.reshape(-1, B), factor_across.reshap...  36.3 us
    select_n x1, other arithmetic, shards(): picked_both = jnp.where(keep_mask, picked_both, 0.0)  29.2 us
  transfers between devices with their start and end apart: 7, of which 7 were waited for; matrix products, arithmetic and copies ran while one was open for 3% of the time, Pallas kernels for 0%

commit v1 on v0

--- a/solution.py
+++ b/solution.py
@@ -8,7 +8,7 @@
 
 def broadcast(x, axis, root):
     mine = lax.axis_index(axis) == root
-    return lax.psum(jnp.where(mine, x, jnp.zeros_like(x)), axis)
+    return jnp.sum(lax.all_gather(jnp.where(mine, x, jnp.zeros_like(x)), axis), axis=0)
 
 
 def inverse_maps(block_maps, count):

time: 1240 us -> 1870 us (1.51)
  waiting for transfers between devices: 664 us -> 1220 us
  other arithmetic: 317 us -> 385 us
  matrix products: 62.2 us -> 88.8 us
  local copies, waits for them, and re-layouts: 160 us -> 135 us
    all_gather x0 -> x6, waiting for transfers between devices: none -> 989 us  [broadcast(): lax.all_gather(jnp.where(mine, x, jnp.zeros_like(x)), axis)]
    psum x6 -> x0, waiting for transfers between devices: 433 us -> none  [broadcast(): return lax.psum(jnp.where(mine, x, jnp.zeros_like(x)), axis)]
    reduce_sum x0 -> x6, other arithmetic: none -> 71.3 us  [broadcast(): jnp.sum(lax.all_gather(jnp.where(mine, x, jnp.zeros_like(x)), axis), axis=0)]
    dot_general x2, matrix products: 36.3 us -> 62.9 us  [shards(): lax.dot_general(factor_factor_column.reshape(-1, B), factor_across.reshap...]
  transfers between devices with their start and end apart: 7 -> 7, of which waited for: 7 -> 7; matrix products, arithmetic and copies ran while one was open for 3% -> 2% of each run, Pallas kernels for 0% -> 0%
where the time goes in v1:
time: 1870 us; the launch traced here: 1860 us
  waiting for transfers between devices  1220 us (65%)
  other arithmetic  385 us (21%)
  local copies, waits for them, and re-layouts  135 us (7%)
  matrix products  88.8 us (5%)
  between operations  19.5 us (1%)
    all_gather x6, waiting for transfers between devices, broadcast(): lax.all_gather(jnp.where(mine, x, jnp.zeros_like(x)), axis)  989 us
    all_to_all x1, waiting for transfers between devices, shards(): lax.all_to_all(buffer, ('row', 'col'), split_axis=0, concat_axis=0, tiled...  231 us
    another operation x29, other arithmetic, shards(): lower_factor = jnp.linalg.cholesky(diagonal)  159 us
    another operation x5, other arithmetic, shards(): jax.scipy.linalg.solve_triangular(lower_factor, column_slab.reshape(-1, B...  79.2 us
    reduce_sum x6, other arithmetic, broadcast(): jnp.sum(lax.all_gather(jnp.where(mine, x, jnp.zeros_like(x)), axis), axis=0)  71.3 us
    dot_general x2, matrix products, shards(): lax.dot_general(factor_factor_column.reshape(-1, B), factor_across.reshap...  62.9 us
  transfers between devices with their start and end apart: 7, of which 7 were waited for; matrix products, arithmetic and copies ran while one was open for 2% of the time, Pallas kernels for 0%

profile of v1, /device:TPU:0, one launch (start us, length us, event | category | flops | bytes accessed | tf_op | source)
XLA Modules:
  0.0 1860.9 jit_solution(4462616231610715015)
XLA Ops:
  7.6 8.1 gather_fusion
  15.6 10.1 broadcast_select_fusion
  25.7 12.2 gather_fusion.1
  38.7 29.2 %fusion = f32[4,8,32,2,16,128]{5,3,2,0,4,1:T(2,128)} fusion(f32[4,8,32,2,16,128]{5,2,1,0,4,3:T(8,128)} %bitcast.141, pred[2,16]{0,1:T(8,128)(4,1)S(1)} %copy.64, pred[4,8,2,16]{2,0,3,1:T(4,128)(4,1)S(1)} %broadcast_and_fusion), kind=kLoop, calls=%fused_computation.10 | loop fusion | flops 8388608 | bytes 33555488 | tf_op jit(solution)/shard_map/jit(_where)/select_n | solution.py:41
  67.9 11.7 all-to-all-start
  81.0 231.0 %all-to-all-done = f32[128,1,32768]{2,1,0:T(1,128)} async-done(((f32[128,1,32768]{2,1,0:T(1,128)}), f32[128,1,32768]{2,1,0:T(1,128)}, u32[]{:S(2)}, u32[]{:S(2)}) %all-to-all-start) | async-done | bytes 16777248 | tf_op jit(solution)/shard_map/all_to_all | solution.py:46
  312.0 11.0 slice_add_fusion
  323.0 12.1 copy.67
  335.1 10.3 reshape.557
  358.7 5.6 copy.85
  364.3 52.6 %all-gather.15.cloned.1.call-done = f32[8,512,1,512]{3,1,2,0:T(8,128)} async-done(((f32[1,512,1,512]{3,1,2,0:T(8,128)}), f32[8,512,1,512]{3,1,2,0:T(8,128)}) %all-gather.15.cloned.1.call-update) | async-done | bytes 8388624 | tf_op jit(solution)/shard_map/all_gather | solution.py:11
  421.9 11.7 cholesky.286
  433.8 9.8 custom-call.27
  444.3 11.9 cholesky.305
  456.3 9.8 custom-call.28
  466.7 11.7 cholesky.326
  479.2 9.8 custom-call.29
  489.6 12.2 cholesky.343
  506.1 8.2 while.8
  514.3 39.3 %custom-call.30 = f32[4,128,128]{1,2,0:T(8,128)S(1)} custom-call(f32[4,128,128]{2,1,0:T(8,128)S(1)} %get-tuple-element.62), custom_call_target="InvertDiagBlocksLowerTriangular" | custom-call | tf_op jit(solution)/shard_map/jit(_solve_triangular)/triangular_solve | solution.py:67
  567.3 5.5 copy.86
  572.8 4.9 select_select_fusion.1
  577.8 369.0 %all-gather.11.cloned.1.call-done = f32[16,4,512,512]{3,2,1,0:T(8,128)} async-done(((f32[1,4,512,512]{3,2,1,0:T(8,128)}), f32[16,4,512,512]{3,2,1,0:T(8,128)}) %all-gather.11.cloned.1.call-update) | async-done | bytes 67108880 | tf_op jit(solution)/shard_map/all_gather | solution.py:11
  946.7 23.1 %reduce_sum.65 = f32[4,512,512]{2,1,0:T(8,128)} reduce(f32[16,4,512,512]{3,2,1,0:T(8,128)} %all-gather.11.cloned.1.call-done, f32[]{:T(128)} %constant.284.clone.1), dimensions={0}, to_apply=%region_11.14 | reduce | flops 15728640 | bytes 71303168 | tf_op jit(solution)/shard_map/reduce_sum | solution.py:11
  974.6 5.4 copy.93
  980.1 79.2 %all-gather.17.cloned.1.call-done = f32[16,512,512]{2,1,0:T(8,128)} async-done(((f32[2,512,512]{2,1,0:T(8,128)}), f32[16,512,512]{2,1,0:T(8,128)}) %all-gather.17.cloned.1.call-update) | async-done | bytes 16777232 | tf_op jit(solution)/shard_map/all_gather | solution.py:11
  1059.2 8.1 reduce_sum.66
  1067.3 31.4 %fusion.2 = f32[4,512,2,512]{3,1,2,0:T(8,128)S(1)} fusion(f32[4,512,2,512]{3,1,2,0:T(8,128)} %copy-done.1, f32[4,512,512]{2,1,0:T(8,128)} %reduce_sum.65, pred[2]{0:T(512)(128)(4,1)S(1)} %get-tuple-element.118, pred[4,2]{1,0:T(4,128)(4,1)S(1)} %get-tuple-element.111, pred[4,2]{1,0:T(4,128)(4,1)S(1)} %get-tuple-element.110, ...), kind=kOutput, calls=%fused_computation.14 | convolution fusion | flops 12893290496 | bytes 27262994 | tf_op jit(solution)/shard_map/dot_general | solution.py:84
  1107.9 5.8 copy.76
  1113.7 40.0 %all-gather.19.cloned.1.call-done = f32[8,512,1,512]{3,1,2,0:T(8,128)} async-done(((f32[1,512,1,512]{3,1,2,0:T(8,128)}), f32[8,512,1,512]{3,1,2,0:T(8,128)}) %all-gather.19.cloned.1.call-update) | async-done | bytes 8388624 | tf_op jit(solution)/shard_map/all_gather | solution.py:11
  1158.8 11.7 cholesky.358
  1170.7 9.8 custom-call.31
  1181.2 11.9 cholesky.377
  1194.4 9.8 custom-call.32
  1204.9 11.7 cholesky.398
  1217.3 9.8 custom-call.33
  1227.7 12.1 cholesky.415
  1243.4 8.1 while.9
  1251.6 39.3 %custom-call.34 = f32[4,128,128]{1,2,0:T(8,128)S(1)} custom-call(f32[4,128,128]{2,1,0:T(8,128)S(1)} %get-tuple-element.63), custom_call_target="InvertDiagBlocksLowerTriangular" | custom-call | tf_op jit(solution)/shard_map/jit(_solve_triangular)/triangular_solve | solution.py:67
  1304.5 5.5 copy.89
  1315.0 369.0 %all-gather.13.cloned.1.call-done = f32[16,4,512,512]{3,2,1,0:T(8,128)} async-done(((f32[1,4,512,512]{3,2,1,0:T(8,128)}), f32[16,4,512,512]{3,2,1,0:T(8,128)}) %all-gather.13.cloned.1.call-update) | async-done | bytes 67108880 | tf_op jit(solution)/shard_map/all_gather | solution.py:11
  1684.0 23.1 %reduce_sum.68 = f32[4,512,512]{2,1,0:T(8,128)} reduce(f32[16,4,512,512]{3,2,1,0:T(8,128)} %all-gather.13.cloned.1.call-done, f32[]{:T(128)} %constant.284.clone.1), dimensions={0}, to_apply=%region_14.18 | reduce | flops 15728640 | bytes 71303168 | tf_op jit(solution)/shard_map/reduce_sum | solution.py:11
  1711.8 5.4 copy.94
  1717.3 79.2 %all-gather.21.cloned.1.call-done = f32[16,512,512]{2,1,0:T(8,128)} async-done(((f32[2,512,512]{2,1,0:T(8,128)}), f32[16,512,512]{2,1,0:T(8,128)}) %all-gather.21.cloned.1.call-update) | async-done | bytes 16777232 | tf_op jit(solution)/shard_map/all_gather | solution.py:11
  1796.5 8.1 reduce_sum.69
  1804.6 31.4 %fusion.4 = f32[4,512,2,512]{3,1,2,0:T(8,128)S(1)} fusion(f32[4,512,2,512]{3,1,2,0:T(8,128)} %copy-done, f32[4,512,512]{2,1,0:T(8,128)} %reduce_sum.68, pred[2]{0:T(512)(128)(4,1)S(1)} %get-tuple-element.124, pred[4,2]{1,0:T(4,128)(4,1)S(1)} %get-tuple-element.109, pred[4,2]{1,0:T(4,128)(4,1)S(1)} %get-tuple-element.108, f32[4,512,512,1]{1,0,2,3:T(4,128)} %bitcast.144, ...), kind=kOutput, calls=%fused_computation.16 | convolution fusion | flops 12893290496 | bytes 27262994 | tf_op jit(solution)/shard_map/dot_general | solution.py:84
  1836.0 12.4 copy.82
  1848.4 5.5 copy.96
  (154 shorter events, 103.0 us)
Async XLA Ops:
  67.9 12.2 copy-start.4
  67.9 244.1 %all-to-all-start = ((f32[128,1,32768]{2,1,0:T(1,128)}), f32[128,1,32768]{2,1,0:T(1,128)}, u32[]{:S(2)}, u32[]{:S(2)}) async-start(f32[128,1,32768]{2,1,0:T(1,128)} %bitcast.140), calls=%async_computation | async-start | bytes 33554432 | tf_op jit(solution)/shard_map/all_to_all | solution.py:46
  79.6 337.3 %all-gather.15.cloned.1.call-start = ((), (), s32[]{:S(2)}) async-start(), calls=%async_computation.3 | async-start | bytes 9437184 | tf_op jit(solution)/shard_map/all_gather | solution.py:11
  349.5 3.4 copy-start.1
  354.0 592.7 %all-gather.11.cloned.1.call-start = ((), (), s32[]{:S(2)}) async-start(), calls=%async_computation.1 | async-start | bytes 71303168 | tf_op jit(solution)/shard_map/all_gather | solution.py:11
  553.6 5.7 copy-start.2
  577.7 481.6 %all-gather.17.cloned.1.call-start = ((), (), s32[]{:S(2)}) async-start(), calls=%async_computation.4 | async-start | bytes 18874368 | tf_op jit(solution)/shard_map/all_gather | solution.py:11
  974.5 179.2 %all-gather.19.cloned.1.call-start = ((), (), s32[]{:S(2)}) async-start(), calls=%async_computation.5 | async-start | bytes 9437184 | tf_op jit(solution)/shard_map/all_gather | solution.py:11
  1098.8 3.4 copy-start
  1103.3 580.7 %all-gather.13.cloned.1.call-start = ((), (), s32[]{:S(2)}) async-start(), calls=%async_computation.2 | async-start | bytes 71303168 | tf_op jit(solution)/shard_map/all_gather | solution.py:11
  1290.9 5.7 copy-start.3
  1314.9 481.6 %all-gather.21.cloned.1.call-start = ((), (), s32[]{:S(2)}) async-start(), calls=%async_computation.6 | async-start | bytes 18874368 | tf_op jit(solution)/shard_map/all_gather | solution.py:11
Sparse Core Ops, SparseCore 0:
  354.1 62.6 all-gather.14
  577.8 368.9 all-gather.10
  974.6 84.5 all-gather.16
  1103.4 50.3 all-gather.18
  1315.0 368.9 all-gather.12
  1711.9 84.5 all-gather.20
